TPU v7x, 32 devices: a whole 2x2x4 slice. The times are simulated.
32 devices in a mesh: seq: 8 (over y, x, core), head: 4 (over z).
Axes of the slice: x: 2, y: 2, z: 4, core: 2. Of those that a mesh axis runs over, the one named last changes fastest.
Arguments:
- mixer_input: bfloat16 [12288, 4096], P('seq', 'head'), may hold values from -6 to 6
- gate_input: bfloat16 [12288, 4096], P('seq', 'head'), may hold values from -6 to 6
- state_maps: bfloat16 [4, 12288, 128], P(None, 'seq'), may hold values from -0.375 to 0.375
- step_size: float32 [2, 64, 12288], P(None, 'head', 'seq'), may hold values from 0.2 to 2
- log_decay: float32 [2, 64, 12288], P(None, 'head', 'seq'), may hold values from -2 to 0
- skip_weight: float32 [64], P('head'), may hold values from 0.5 to 1.5
- doc_ids: int32 [12288], P('seq'), may hold values from 0 to 3, never falling along the last dimension, each value on 1 to 6144 neighbouring positions
- norm_gain: float32 [4096], P('head'), may hold values from 0.1 to 1.9
Outputs:
- mixed: bfloat16 [12288, 4096], P('seq', 'head')
Inputs may be any that keep to these rules, and one draw needn't show every extreme that they name: `doc_ids`: ids never fall along the sequence; each of the 4 documents holds 1 to 6144 tokens, one exactly 6144.
All inputs are finite; a program needn't handle non-finite values.
Results may differ from a plain program's by a relative error of at most 0.0054.
Values sent between devices are 32-bit elements; how exact they have to be, the bound alone decides.
A program may use at most 256 MiB of HBM per device.

v0:
```python
import jax
import jax.numpy as jnp
from jax import lax
from jax.sharding import PartitionSpec as P

BLOCK = 128


def prefix(part, axis, combine, identity, reverse):
    count = lax.axis_size(axis)
    place = lax.axis_index(axis)
    ahead = count - 1 - place if reverse else place
    gathered = jax.tree.map(lambda a: lax.all_gather(a, axis), part)
    state = jax.tree.map(lambda a, e: jnp.zeros_like(a) + jnp.asarray(e, a.dtype), part, identity)

    def one(step, state):
        source = count - 1 - step if reverse else step
        return combine(
            state, jax.tree.map(lambda a: lax.dynamic_index_in_dim(a, source, 0, False), gathered)
        )

    return lax.fori_loop(0, ahead, one, state)


def combine(earlier, later):
    decay_first, state_first, enter_first, leave_first = earlier
    decay_second, state_second, enter_second, leave_second = later
    keeping = ((leave_first == enter_second) | (enter_first < 0.0) | (enter_second < 0.0)).astype(
        jnp.float32
    )
    carried = decay_second * keeping
    return (
        carried * decay_first,
        state_second + carried[:, None, None] * state_first,
        jnp.where(enter_first < 0.0, enter_second, enter_first),
        jnp.where(leave_second < 0.0, leave_first, leave_second),
    )


def local_pass(blocks_x, b_rows, c_rows, decay_rows, step_rows, doc_rows):
    block_count = blocks_x.shape[0]
    head_count = decay_rows.shape[0]
    b_blocks = b_rows.reshape(block_count, BLOCK, -1)
    c_blocks = c_rows.reshape(block_count, BLOCK, -1)
    cumulative = jnp.cumsum(decay_rows.reshape(head_count, block_count, BLOCK), axis=2)
    step_blocks = step_rows.reshape(head_count, block_count, BLOCK)
    doc_blocks = doc_rows.reshape(block_count, BLOCK)
    scores = jnp.einsum("btn,bsn->bts", c_blocks, b_blocks, preferred_element_type=jnp.float32)
    places = jnp.arange(BLOCK)
    strict = (places[:, None] > places[None, :])[None] & (
        doc_blocks[:, :, None] == doc_blocks[:, None, :]
    )
    spread = jnp.where(strict[None], cumulative[:, :, :, None] - cumulative[:, :, None, :], 0.0)
    weights = jnp.where(
        strict[None], scores[None] * jnp.exp(spread) * step_blocks[:, :, None, :], 0.0
    )
    weights = weights.astype(jnp.bfloat16)
    inside_out = jnp.einsum(
        "hbts,bshp->bthp", weights, blocks_x, preferred_element_type=jnp.float32
    )
    last_ids = doc_blocks[:, -1]
    same_end = doc_blocks == last_ids[:, None]
    to_end = jnp.where(
        same_end[None], jnp.exp(cumulative[:, :, -1:] - cumulative) * step_blocks, 0.0
    )
    weighted_b = (b_blocks.astype(jnp.float32)[None] * to_end[..., None]).astype(jnp.bfloat16)
    local_states = jnp.einsum(
        "hbsn,bshp->bhnp", weighted_b, blocks_x, preferred_element_type=jnp.float32
    )
    prior_ids = jnp.concatenate([doc_rows[:1], last_ids[:-1]])
    block_decay = (
        jnp.exp(cumulative[:, :, -1]).T * (last_ids == prior_ids).astype(jnp.float32)[:, None]
    )

    def advance(carried_pair, block_item):
        state_now, factor_now = carried_pair
        local_now, decay_now = block_item
        return (
            (decay_now[:, None, None] * state_now + local_now, factor_now * decay_now),
            (state_now, factor_now),
        )

    start_state = jnp.zeros(local_states.shape[1:], jnp.float32)
    start_factor = jnp.ones((head_count,), jnp.float32)
    (final_state, total_decay), (starts, factors) = lax.scan(
        advance, (start_state, start_factor), (local_states, block_decay)
    )
    summary = (
        total_decay,
        final_state,
        doc_rows[:1].astype(jnp.float32),
        doc_rows[-1:].astype(jnp.float32),
    )
    return (inside_out, cumulative, starts, factors, prior_ids, summary)


def finish(c_rows, doc_rows, parts, incoming):
    inside_out, cumulative, starts, factors, prior_ids, summary = parts
    block_count = starts.shape[0]
    matching = (incoming[3] == doc_rows[:1].astype(jnp.float32)).astype(jnp.float32)
    arriving = incoming[1] * matching[:, None, None]
    entering = (starts + factors[:, :, None, None] * arriving[None]).astype(jnp.bfloat16)
    c_blocks = c_rows.reshape(block_count, BLOCK, -1)
    carried = jnp.einsum("btn,bhnp->bthp", c_blocks, entering, preferred_element_type=jnp.float32)
    doc_blocks = doc_rows.reshape(block_count, BLOCK)
    same_doc = (doc_blocks == prior_ids[:, None]).astype(jnp.float32)
    carry_reach = jnp.exp(cumulative).transpose(1, 2, 0) * same_doc[:, :, None]
    return inside_out + carried * carry_reach[..., None]


def local(
    mixer_input, gate_input, state_maps, step_size, log_decay, skip_weight, doc_ids, norm_gain
):
    tokens = mixer_input.shape[0]
    head_count = step_size.shape[1]
    head_width = mixer_input.shape[1] // head_count
    state_dim = state_maps.shape[2]
    block_count = tokens // BLOCK
    per_token = mixer_input.reshape(tokens, head_count, head_width)
    forward_x = per_token.reshape(block_count, BLOCK, head_count, head_width)
    backward_x = per_token[::-1].reshape(block_count, BLOCK, head_count, head_width)
    reversed_docs = doc_ids[::-1]
    reversed_c = state_maps[3][::-1]
    fwd_parts = local_pass(
        forward_x, state_maps[0], state_maps[1], log_decay[0], step_size[0], doc_ids
    )
    bwd_parts = local_pass(
        backward_x,
        state_maps[2][::-1],
        reversed_c,
        log_decay[1][:, ::-1],
        step_size[1][:, ::-1],
        reversed_docs,
    )
    fwd_sum = fwd_parts[5]
    bwd_sum = bwd_parts[5]
    neutral = (
        jnp.ones((head_count,), jnp.float32),
        jnp.zeros((head_count, state_dim, head_width), jnp.float32),
        -jnp.ones((1,), jnp.float32),
        -jnp.ones((1,), jnp.float32),
    )
    fwd_in = prefix(
        (fwd_sum[0], fwd_sum[1], fwd_sum[2], fwd_sum[3]), "seq", combine, neutral, False
    )
    bwd_in = prefix((bwd_sum[0], bwd_sum[1], bwd_sum[2], bwd_sum[3]), "seq", combine, neutral, True)
    forward_out = finish(state_maps[1], doc_ids, fwd_parts, fwd_in).reshape(
        tokens, head_count, head_width
    )
    backward_out = finish(reversed_c, reversed_docs, bwd_parts, bwd_in).reshape(
        tokens, head_count, head_width
    )[::-1]
    combined = (
        forward_out + backward_out + skip_weight[None, :, None] * per_token.astype(jnp.float32)
    )
    gate_wide = gate_input.astype(jnp.float32).reshape(tokens, head_count, head_width)
    gated_out = (combined * jax.nn.silu(gate_wide)).reshape(tokens, head_count * head_width)
    partial_squares = jnp.sum(gated_out * gated_out, axis=1)
    square_total = lax.psum(partial_squares, "head")
    channels = lax.axis_size("head") * head_count * head_width
    inverse_rms = lax.rsqrt(square_total / channels + 1e-05)
    return (gated_out * inverse_rms[:, None] * norm_gain[None, :]).astype(jnp.bfloat16)


def solution(mesh):
    return jax.shard_map(
        local,
        mesh=mesh,
        in_specs=(
            P("seq", "head"),
            P("seq", "head"),
            P(None, "seq", None),
            P(None, "head", "seq"),
            P(None, "head", "seq"),
            P("head"),
            P("seq"),
            P("head"),
        ),
        out_specs=P("seq", "head"),
        check_vma=False,
    )
```

profile of v0, /device:TPU:0, one launch (start us, length us, event | category | flops | bytes accessed | tf_op | source)
XLA Modules:
  0.0 315.6 jit_solution(17336573197923804926)
XLA Ops:
  9.6 1.5 slice_reduce_fusion.5
  13.0 2.4 fusion.58
  15.4 4.6 %copy.124 = bf16[1536,1024]{0,1:T(8,128)(2,1)} copy(bf16[1536,1024]{1,0:T(8,128)(2,1)} %param.16) | data formatting | bytes 6291456 | tf_op args[0]
  20.0 4.5 %reduce_window_sum.17 = f32[16,12,128]{2,1,0:T(8,128)S(1)} reduce-window(f32[16,12,128]{2,1,0:T(8,128)S(1)} %reshape_squeeze.13, f32[]{:T(128)} %constant.111.clone.1), window={size=1x1x128 pad=0_0x0_0x127_0}, to_apply=%region_0.0 | reduce-window | flops 3121152 | bytes 196612 | tf_op jit(solution)/shard_map/jit(cumsum)/reduce_window_sum | solution.py:45
  26.4 6.9 %reshape_reshape.3 = bf16[12,128,16,64]{1,0,3,2:T(8,128)(2,1)} reshape(bf16[1536,1024]{0,1:T(8,128)(2,1)} %copy.124) | data formatting | bytes 6291456 | tf_op jit(solution)/shard_map/reshape;reshape | solution.py:120
  34.1 10.4 %fusion.16 = f32[12,16,128,64]{3,2,1,0:T(8,128)} fusion(f32[16,12,128]{2,0,1:T(8,128)S(1)} %copy.126, f32[12,128,128]{2,1,0:T(8,128)S(1)} %convert_element_type.77, bf16[12,128,16,64]{1,0,3,2:T(8,128)(2,1)} %reshape_reshape.3), kind=kOutput, calls=%fused_computation.42 | convolution fusion | flops 408944640 | bytes 10321920 | tf_op jit(solution)/shard_map/hbsn,bshp->bhnp/dot_general | solution.py:67
  44.5 6.1 %broadcast.140.clone.1 = f32[12,16,128,64]{3,2,1,0:T(8,128)} broadcast(f32[]{:T(128)} %constant.111.clone.1), dimensions={} | broadcast | bytes 6291460 | tf_op jit(solution)/shard_map/broadcast.7
  50.6 30.8 %while.70 = (s32[]{:T(128)}, f32[16,128,64]{2,1,0:T(8,128)S(1)}, f32[16]{0:T(128)S(1)}, f32[12,16,128,64]{3,2,1,0:T(8,128)}, f32[12,16]{1,0:T(8,128)S(1)}, /*ind...) while((s32[]{:T(128)}, f32[16,128,64]{2,1,0:T(8,128)S(1)}, ...), condition=%wide.region_2.3_spmd.clone, body=%wide.region_1.2_spmd.clone.sunk | while | flops 524323 | bytes 3146869 | solution.py:85
  69.7 1.4 bitcast_add_fusion.11
  72.3 1.4 bitcast_add_fusion.11
  74.8 1.4 bitcast_add_fusion.11
  83.8 4.6 %reduce_window_sum.18 = f32[16,12,128]{2,1,0:T(8,128)S(1)} reduce-window(f32[16,12,128]{2,1,0:T(8,128)S(1)} %reshape.215, f32[]{:T(128)} %constant.111.clone.1), window={size=1x1x128 pad=0_0x0_0x127_0}, to_apply=%region_5.6 | reduce-window | flops 3121152 | bytes 196612 | tf_op jit(solution)/shard_map/jit(cumsum)/reduce_window_sum | solution.py:45
  92.1 8.8 %rev.26 = bf16[1536,16,64]{0,2,1:T(8,128)(2,1)} reverse(bf16[1536,16,64]{0,2,1:T(8,128)(2,1)} %bitcast.170), dimensions={0} | reverse | bytes 6291456 | tf_op jit(solution)/shard_map/rev | solution.py:121
  100.8 1.5 convert_reduce_fusion
  102.4 10.3 %fusion.18 = f32[12,16,128,64]{3,2,1,0:T(8,128)} fusion(f32[16,12,128]{2,0,1:T(8,128)} %copy.140, f32[12,128,128]{2,1,0:T(8,128)S(1)} %convert_element_type.84, bf16[1536,16,64]{0,2,1:T(8,128)(2,1)} %rev.26), kind=kOutput, calls=%fused_computation.44 | convolution fusion | flops 408944640 | bytes 10321920 | tf_op jit(solution)/shard_map/hbsn,bshp->bhnp/dot_general | solution.py:67
  112.7 6.1 %broadcast.140.clone = f32[12,16,128,64]{3,2,1,0:T(8,128)} broadcast(f32[]{:T(128)} %constant.111.clone.1), dimensions={} | broadcast | bytes 6291460 | tf_op jit(solution)/shard_map/broadcast.7
  118.8 30.9 %while.71 = (s32[]{:T(128)}, f32[16,128,64]{2,1,0:T(8,128)S(1)}, f32[16]{0:T(128)S(1)}, f32[12,16,128,64]{3,2,1,0:T(8,128)}, f32[12,16]{1,0:T(8,128)S(1)}, /*ind...) while((s32[]{:T(128)}, f32[16,128,64]{2,1,0:T(8,128)S(1)}, ...), condition=%wide.region_7.8_spmd.clone, body=%wide.region_6.7_spmd.clone.sunk | while | flops 524323 | bytes 3146869 | solution.py:85
  132.9 1.4 bitcast_add_fusion.12
  135.4 1.4 bitcast_add_fusion.12
  155.5 15.5 %all-reduce.4 = (f32[128]{0:T(128)S(1)}, f32[8]{0:T(128)S(1)}, f32[8]{0:T(128)S(1)}, f32[128]{0:T(128)S(1)}) all-reduce(f32[128]{0:T(128)S(1)} %dynamic-update-slice.3, f32[8]{0:T(128)S(1)} %convert_dynamic-update-slice_fusion, f32[8]{0:T(128)S(1)} %convert_dynamic-update-slice_fusion.1, ...), channel_id=7, replica_groups=mesh['seq'=8,'head'=4] {'seq'}, use_global_device_ids=true, to_apply=%add.3 | all-reduce | flops 272 | bytes 2176
  172.8 5.0 %copy.149 = bf16[1536,1024]{0,1:T(8,128)(2,1)} copy(bf16[1536,1024]{1,0:T(8,128)(2,1)} %param.17) | data formatting | bytes 6291456 | tf_op args[1]
  179.2 9.2 %fusion.10 = f32[12,16,128,64]{2,3,1,0:T(8,128)} fusion(f32[16,12,128]{2,0,1:T(8,128)S(1)} %copy.123, f32[16,12,128]{2,0,1:T(8,128)S(1)} %copy.121, f32[12,128,128]{2,1,0:T(8,128)S(1)} %fusion.63, pred[12,128,128]{2,1,0:T(8,128)(4,1)S(1)} %get-tuple-element.557, bf16[12,128,16,64]{1,0,3,2:T(8,128)(2,1)} %reshape_reshape.3), kind=kOutput, calls=%fused_computation.36 | convolution fusion | flops 421527552 | bytes 10616832 | tf_op jit(solution)/shard_map/hbts,bshp->bthp/dot_general | solution.py:58
  188.4 8.6 %fusion.11 = f32[12,16,128,64]{2,3,1,0:T(8,128)} fusion(f32[16,12,128]{2,0,1:T(8,128)S(1)} %copy_bitcast_fusion.1, f32[16,12,128]{2,0,1:T(8,128)S(1)} %copy.135, f32[12,128,128]{2,1,0:T(8,128)S(1)} %fusion.64, pred[12,128,128]{2,1,0:T(8,128)(4,1)S(1)} %get-tuple-element.558, bf16[1536,16,64]{0,2,1:T(8,128)(2,1)S(1)} %copy-done.3), kind=kOutput, calls=%fused_computation.37 | convolution fusion | flops 421527552 | bytes 10616832 | tf_op jit(solution)/shard_map/hbts,bshp->bthp/dot_general | solution.py:58
  198.2 40.0 %while.69 = (s32[]{:T(128)}, f32[16,128,64]{2,1,0:T(8,128)S(1)}, f32[1]{0:T(128)}, f32[1]{0:T(128)}, s32[]{:T(128)}, /*index=5*/f32[8,16,128,64]{2,3,1,0:T(8,128...) while((s32[]{:T(128)}, f32[16,128,64]{2,1,0:T(8,128)S(1)}, ...), condition=%wide.region_9.10_spmd, body=%wide.region_8.9_spmd.sunk | while | flops 262175 | bytes 3670492 | solution.py:22
  238.3 12.6 %fusion.24 = f32[12,16,8,8,128]{4,3,2,1,0:T(8,128)} fusion(f32[12,16,128,64]{2,3,1,0:T(8,128)} %fusion.11, f32[12,128,16]{1,2,0:T(8,128)S(1)} %copy-done.9, bf16[12,128,128,1]{2,1,3,0:T(8,128)(2,1)S(1)} %bitcast.179, f32[12,16,128,64]{3,2,1,0:T(8,128)} %get-tuple-element.305, f32[16,128,64]{2,1,0:T(8,128)S(1)} %broadcast_multiply_fusion, ...), kind=kOutput, calls=%fused_computation.54 | convolution fusion | flops 410517504 | bytes 19890944 | tf_op jit(solution)/shard_map/btn,bhnp->bthp/dot_general | solution.py:104
  251.0 6.2 %copy.179 = f32[12,16,8,8,128]{4,3,0,2,1:T(8,128)} copy(f32[12,16,8,8,128]{4,3,2,1,0:T(8,128)} %fusion.24) | data formatting | bytes 12582912 | tf_op jit(solution)/shard_map/reshape | solution.py:150
  257.2 10.5 %rev.27 = f32[1536,16,64]{0,2,1:T(8,128)} reverse(f32[1536,16,64]{0,2,1:T(8,128)} %bitcast.171), dimensions={0} | reverse | bytes 12582912 | tf_op jit(solution)/shard_map/rev | solution.py:150
  268.7 13.0 %fusion.26 = f32[12,16,8,8,128]{4,3,2,1,0:T(8,128)} fusion(f32[12,16,128,64]{2,3,1,0:T(8,128)} %fusion.10, f32[12,128,16]{1,2,0:T(8,128)} %copy.133, bf16[12,128,128,1]{2,1,3,0:T(8,128)(2,1)S(1)} %bitcast.177, f32[12,16,128,64]{3,2,1,0:T(8,128)} %get-tuple-element.299, f32[16,128,64]{2,1,0:T(8,128)} %broadcast_multiply_fusion.1, f32[12,16]{1,0:T(8,128)S(1)} %copy-done.11), kind=kOutput, calls=%fused_computation.57 | convolution fusion | flops 410517504 | bytes 19890944 | tf_op jit(solution)/shard_map/btn,bhnp->bthp/dot_general | solution.py:104
  281.8 8.6 %multiply_reduce_fusion = (f32[1536]{0:T(1024)S(1)}, f32[1536,16,64]{0,2,1:T(8,128)}) fusion(f32[16]{0:T(128)S(1)} %copy-done.16, f32[1536,16,64]{0,2,1:T(8,128)} %rev.27, f32[12,16,8,8,128]{4,3,2,1,0:T(8,128)} %fusion.26, bf16[1536,1024]{0,1:T(8,128)(2,1)} %copy.149, bf16[1536,1024]{0,1:T(8,128)(2,1)S(1)} %copy-done.2), kind=kLoop, calls=%fused_computation.58 | loop fusion | flops 18872832 | bytes 25172032 | tf_op jit(solution)/shard_map/reduce_sum | solution.py:158
  290.3 12.1 %psum.7 = f32[1536]{0:T(1024)S(1)} all-reduce(f32[1536]{0:T(1024)S(1)} %get-tuple-element.537), channel_id=1, replica_groups=mesh['seq'=8,'head'=4] {'head'}, use_global_device_ids=true, to_apply=%region_11.12 | all-reduce | flops 1536 | bytes 12288 | tf_op jit(solution)/shard_map/psum | solution.py:159
  302.5 3.4 %fusion.22 = bf16[1536,1024]{0,1:T(8,128)(2,1)S(1)} fusion(f32[1536,16,64]{0,2,1:T(8,128)} %get-tuple-element.538, f32[1024]{0:T(1024)S(1)} %copy-done.15, f32[1536]{0:T(1024)S(1)} %add_rsqrt_fusion), kind=kLoop, calls=%fused_computation.51 | loop fusion | flops 4718592 | bytes 9447424 | tf_op jit(solution)/shard_map/convert_element_type | solution.py:162
  305.9 2.9 copy.150
  (234 shorter events, 93.4 us)
Async XLA Ops:
  6.5 18.9 %copy-start.8 = (s32[1536]{0:T(1024)S(1)}, s32[1536]{0:T(1024)}, u32[]{:S(2)}) copy-start(s32[1536]{0:T(1024)} %param.22) | copy-start | bytes 18436
  6.5 190.5 %all-gather.9.cloned.1.call-start = ((), (), s32[]{:S(2)}) async-start(), calls=%async_computation | async-start | bytes 4718592 | tf_op jit(solution)/shard_map/all_gather | solution.py:13
  50.6 41.0 %copy-start.5 = (bf16[1536,128]{1,0:T(8,128)(2,1)S(1)}, bf16[1536,128]{1,0:T(8,128)(2,1)}, u32[]{:S(2)}) copy-start(bf16[1536,128]{1,0:T(8,128)(2,1)} %get-tuple-element.547) | copy-start | bytes 1179652
  81.4 1.4 copy-start.12
  81.4 10.2 %copy-start.10 = (f32[12,16]{1,0:T(8,128)}, f32[12,16]{1,0:T(8,128)S(1)}, u32[]{:S(2)}) copy-start(f32[12,16]{1,0:T(8,128)S(1)} %get-tuple-element.300) | copy-start | bytes 2308
  82.6 114.6 %all-gather.11.cloned.1.call-start = ((), (), s32[]{:S(2)}) async-start(), calls=%async_computation.1 | async-start | bytes 4718592 | tf_op jit(solution)/shard_map/all_gather | solution.py:13
  112.7 6.1 %copy-start.14 = (f32[16]{0:T(128)S(1)}, f32[16]{0:T(128)}, u32[]{:S(2)}) copy-start(f32[16]{0:T(128)} %custom-call.3) | copy-start | bytes 196
  118.8 33.5 %copy-start.17 = (u32[32]{0:T(128)S(1)}, u32[32]{0:T(128)}, u32[]{:S(2)}) copy-start(u32[32]{0:T(128)} %constant.122) | copy-start | bytes 388
  118.8 34.9 %copy-start.13 = (f32[16]{0:T(128)S(1)}, f32[16]{0:T(128)}, u32[]{:S(2)}) copy-start(f32[16]{0:T(128)} %copy-done.12) | copy-start | bytes 196
  118.8 52.2 %copy-start.6 = (f32[12,128,16]{1,0,2:T(8,128)S(1)}, f32[12,128,16]{1,0,2:T(8,128)}, u32[]{:S(2)}) copy-start(f32[12,128,16]{1,0,2:T(8,128)} %get-tuple-element.553) | copy-start | bytes 294916
  118.8 53.0 %copy-start.7 = (f32[12,128,16]{1,0,2:T(8,128)S(1)}, f32[12,128,16]{1,0,2:T(8,128)}, u32[]{:S(2)}) copy-start(f32[12,128,16]{1,0,2:T(8,128)} %get-tuple-element.556) | copy-start | bytes 294916
  118.8 53.6 %copy-start.4 = (bf16[1536,128]{1,0:T(8,128)(2,1)S(1)}, bf16[1536,128]{1,0:T(8,128)(2,1)}, u32[]{:S(2)}) copy-start(bf16[1536,128]{1,0:T(8,128)(2,1)} %get-tuple-element.548) | copy-start | bytes 1179652
  179.2 9.2 %copy-start.3 = (bf16[1536,16,64]{0,2,1:T(8,128)(2,1)S(1)}, bf16[1536,16,64]{0,2,1:T(8,128)(2,1)}, u32[]{:S(2)}) copy-start(bf16[1536,16,64]{0,2,1:T(8,128)(2,1)} %rev.26) | copy-start | bytes 9437188
  197.1 0.9 copy-start
  198.2 40.1 %copy-start.9 = (f32[12,128,16]{1,2,0:T(8,128)S(1)}, f32[12,128,16]{1,2,0:T(8,128)}, u32[]{:S(2)}) copy-start(f32[12,128,16]{1,2,0:T(8,128)} %copy.147) | copy-start | bytes 294916
  257.2 10.5 %copy-start.1 = (f32[16,128,64]{2,1,0:T(8,128)S(1)}, f32[16,128,64]{2,1,0:T(8,128)}, u32[]{:S(2)}) copy-start(f32[16,128,64]{2,1,0:T(8,128)} %copy-done) | copy-start | bytes 1572868
  257.2 11.6 %copy-start.11 = (f32[12,16]{1,0:T(8,128)S(1)}, f32[12,16]{1,0:T(8,128)}, u32[]{:S(2)}) copy-start(f32[12,16]{1,0:T(8,128)} %copy-done.10) | copy-start | bytes 2308
  268.7 13.0 %copy-start.2 = (bf16[1536,1024]{0,1:T(8,128)(2,1)S(1)}, bf16[1536,1024]{0,1:T(8,128)(2,1)}, u32[]{:S(2)}) copy-start(bf16[1536,1024]{0,1:T(8,128)(2,1)} %copy.124) | copy-start | bytes 9437188
  268.7 13.0 %copy-start.16 = (f32[16]{0:T(128)S(1)}, f32[16]{0:T(128)}, u32[]{:S(2)}) copy-start(f32[16]{0:T(128)} %param.21) | copy-start | bytes 196
  281.8 20.7 %copy-start.15 = (f32[1024]{0:T(1024)S(1)}, f32[1024]{0:T(1024)}, u32[]{:S(2)}) copy-start(f32[1024]{0:T(1024)} %param.23) | copy-start | bytes 12292
Sparse Core Ops, SparseCore 0:
  82.7 39.4 all-gather.8
  151.1 39.5 all-gather.10
where the time goes:
time: 319 us; the launch traced here: 316 us
  local copies, waits for them, and re-layouts  91.5 us (29%)
  other arithmetic  91.5 us (29%)
  matrix products  65 us (20%)
  blocking collectives  27.6 us (9%)
  loops' own time  24.3 us (8%)
  between operations  15.6 us (5%)
    add x24, other arithmetic, advance(): decay_now[:, None, None] * state_now + local_now  34 us
    dynamic_update_slice x24, other arithmetic, local_pass(): lax.scan(advance, (start_state, start_factor), (local_states, block_decay))  25.9 us
    dot_general x2, matrix products, finish(): jnp.einsum('btn,bhnp->bthp', c_blocks, entering, preferred_element_type=j...  25.7 us
    another operation x2, loops' own time, prefix(): return lax.fori_loop(0, ahead, one, state)  23.8 us
    dot_general x2, matrix products, local_pass(): jnp.einsum('hbsn,bshp->bhnp', weighted_b, blocks_x, preferred_element_typ...  20.7 us
    dot_general x2, matrix products, local_pass(): jnp.einsum('hbts,bshp->bthp', weights, blocks_x, preferred_element_type=j...  17.8 us
    unnamed x1, blocking collectives  15.5 us
    dynamic_slice x21, local copies, waits for them, and re-layouts, one(): lax.dynamic_index_in_dim(a, source, 0, False)  14.6 us
  transfers between devices with their start and end apart: 2, of which 0 were waited for; matrix products, arithmetic and copies ran while one was open for 31% of the time, Pallas kernels for 0%

commit v1 on v0

--- a/solution.py
+++ b/solution.py
@@ -156,7 +156,8 @@
     gate_wide = gate_input.astype(jnp.float32).reshape(tokens, head_count, head_width)
     gated_out = (combined * jax.nn.silu(gate_wide)).reshape(tokens, head_count * head_width)
     partial_squares = jnp.sum(gated_out * gated_out, axis=1)
-    square_total = lax.psum(partial_squares, "head")
+    big = lax.all_gather(partial_squares, "head")
+    square_total = jnp.sum(big, axis=0)
     channels = lax.axis_size("head") * head_count * head_width
     inverse_rms = lax.rsqrt(square_total / channels + 1e-05)
     return (gated_out * inverse_rms[:, None] * norm_gain[None, :]).astype(jnp.bfloat16)

time: 319 us -> 333 us (1.044)
  other arithmetic: 91.5 us -> 108 us
    add x7, other arithmetic: 1.53 us -> 16.6 us  [combine(): state_second + carried[:, None, None] * state_first]
    all_gather x0 -> x1, blocking collectives: none -> 13.3 us  [local(): big = lax.all_gather(partial_squares, 'head')]
    psum x1 -> x0, blocking collectives: 12.1 us -> none  [local(): square_total = lax.psum(partial_squares, 'head')]
    unnamed x47 -> x44, local copies, waits for them, and re-layouts: 11.8 us -> 10.9 us
  transfers between devices with their start and end apart: 2 -> 2, of which waited for: 0 -> 0; matrix products, arithmetic and copies ran while one was open for 31% -> 29% of each run, Pallas kernels for 0% -> 0%
where the time goes in v1:
time: 333 us; the launch traced here: 330 us
  other arithmetic  108 us (32%)
  local copies, waits for them, and re-layouts  90.8 us (27%)
  matrix products  65.2 us (20%)
  blocking collectives  28.8 us (9%)
  loops' own time  21.7 us (7%)
  between operations  15.6 us (5%)
    add x24, other arithmetic, advance(): decay_now[:, None, None] * state_now + local_now  34 us
    dynamic_update_slice x24, other arithmetic, local_pass(): lax.scan(advance, (start_state, start_factor), (local_states, block_decay))  25.8 us
    dot_general x2, matrix products, finish(): jnp.einsum('btn,bhnp->bthp', c_blocks, entering, preferred_element_type=j...  25.7 us
    another operation x2, loops' own time, prefix(): return lax.fori_loop(0, ahead, one, state)  21.2 us
    dot_general x2, matrix products, local_pass(): jnp.einsum('hbsn,bshp->bhnp', weighted_b, blocks_x, preferred_element_typ...  20.8 us
    dot_general x2, matrix products, local_pass(): jnp.einsum('hbts,bshp->bthp', weights, blocks_x, preferred_element_type=j...  17.9 us
    add x7, other arithmetic, combine(): state_second + carried[:, None, None] * state_first  16.6 us
    unnamed x1, blocking collectives  15.5 us
  transfers between devices with their start and end apart: 2, of which 0 were waited for; matrix products, arithmetic and copies ran while one was open for 29% of the time, Pallas kernels for 0%

profile of v1, /device:TPU:0, one launch (start us, length us, event | category | flops | bytes accessed | tf_op | source)
XLA Modules:
  0.0 329.9 jit_solution(6848693730752550988)
XLA Ops:
  13.0 2.4 fusion.58
  15.4 4.6 %copy.124 = bf16[1536,1024]{0,1:T(8,128)(2,1)} copy(bf16[1536,1024]{1,0:T(8,128)(2,1)} %param.16) | data formatting | bytes 6291456 | tf_op args[0]
  20.0 4.5 %reduce_window_sum.17 = f32[16,12,128]{2,1,0:T(8,128)S(1)} reduce-window(f32[16,12,128]{2,1,0:T(8,128)S(1)} %reshape_squeeze.13, f32[]{:T(128)} %constant.111.clone.1), window={size=1x1x128 pad=0_0x0_0x127_0}, to_apply=%region_0.0 | reduce-window | flops 3121152 | bytes 196612 | tf_op jit(solution)/shard_map/jit(cumsum)/reduce_window_sum | solution.py:45
  26.5 6.9 %reshape_reshape.3 = bf16[12,128,16,64]{1,0,3,2:T(8,128)(2,1)} reshape(bf16[1536,1024]{0,1:T(8,128)(2,1)} %copy.124) | data formatting | bytes 6291456 | tf_op jit(solution)/shard_map/reshape;reshape | solution.py:120
  34.3 10.5 %fusion.16 = f32[12,16,128,64]{3,2,1,0:T(8,128)} fusion(f32[16,12,128]{2,0,1:T(8,128)S(1)} %copy.126, f32[12,128,128]{2,1,0:T(8,128)S(1)} %convert_element_type.77, bf16[12,128,16,64]{1,0,3,2:T(8,128)(2,1)} %reshape_reshape.3), kind=kOutput, calls=%fused_computation.42 | convolution fusion | flops 408944640 | bytes 10321920 | tf_op jit(solution)/shard_map/hbsn,bshp->bhnp/dot_general | solution.py:67
  44.8 6.1 %broadcast.147.clone.1 = f32[12,16,128,64]{3,2,1,0:T(8,128)} broadcast(f32[]{:T(128)} %constant.111.clone.1), dimensions={} | broadcast | bytes 6291460 | tf_op jit(solution)/shard_map/broadcast.7
  50.9 30.8 %while.70 = (s32[]{:T(128)}, f32[16,128,64]{2,1,0:T(8,128)S(1)}, f32[16]{0:T(128)S(1)}, f32[12,16,128,64]{3,2,1,0:T(8,128)}, f32[12,16]{1,0:T(8,128)S(1)}, /*ind...) while((s32[]{:T(128)}, f32[16,128,64]{2,1,0:T(8,128)S(1)}, ...), condition=%wide.region_2.3_spmd.clone, body=%wide.region_1.2_spmd.clone.sunk | while | flops 524323 | bytes 3146869 | solution.py:85
  84.0 4.6 %reduce_window_sum.18 = f32[16,12,128]{2,1,0:T(8,128)S(1)} reduce-window(f32[16,12,128]{2,1,0:T(8,128)S(1)} %reshape.219, f32[]{:T(128)} %constant.111.clone.1), window={size=1x1x128 pad=0_0x0_0x127_0}, to_apply=%region_5.6 | reduce-window | flops 3121152 | bytes 196612 | tf_op jit(solution)/shard_map/jit(cumsum)/reduce_window_sum | solution.py:45
  92.3 8.6 %rev.26 = bf16[1536,16,64]{0,2,1:T(8,128)(2,1)} reverse(bf16[1536,16,64]{0,2,1:T(8,128)(2,1)} %bitcast.170), dimensions={0} | reverse | bytes 6291456 | tf_op jit(solution)/shard_map/rev | solution.py:121
  102.4 10.4 %fusion.18 = f32[12,16,128,64]{3,2,1,0:T(8,128)} fusion(f32[16,12,128]{2,0,1:T(8,128)} %copy.140, f32[12,128,128]{2,1,0:T(8,128)S(1)} %convert_element_type.84, bf16[1536,16,64]{0,2,1:T(8,128)(2,1)} %rev.26), kind=kOutput, calls=%fused_computation.44 | convolution fusion | flops 408944640 | bytes 10321920 | tf_op jit(solution)/shard_map/hbsn,bshp->bhnp/dot_general | solution.py:67
  112.8 6.1 %broadcast.147.clone = f32[12,16,128,64]{3,2,1,0:T(8,128)} broadcast(f32[]{:T(128)} %constant.111.clone.1), dimensions={} | broadcast | bytes 6291460 | tf_op jit(solution)/shard_map/broadcast.7
  118.9 30.8 %while.71 = (s32[]{:T(128)}, f32[16,128,64]{2,1,0:T(8,128)S(1)}, f32[16]{0:T(128)S(1)}, f32[12,16,128,64]{3,2,1,0:T(8,128)}, f32[12,16]{1,0:T(8,128)S(1)}, /*ind...) while((s32[]{:T(128)}, f32[16,128,64]{2,1,0:T(8,128)S(1)}, ...), condition=%wide.region_7.8_spmd.clone, body=%wide.region_6.7_spmd.clone.sunk | while | flops 524323 | bytes 3146869 | solution.py:85
  155.4 15.5 %all-reduce.4 = (f32[128]{0:T(128)S(1)}, f32[8]{0:T(128)S(1)}, f32[8]{0:T(128)S(1)}, f32[128]{0:T(128)S(1)}) all-reduce(f32[128]{0:T(128)S(1)} %dynamic-update-slice.3, f32[8]{0:T(128)S(1)} %convert_dynamic-update-slice_fusion, f32[8]{0:T(128)S(1)} %convert_dynamic-update-slice_fusion.1, ...), channel_id=7, replica_groups=mesh['seq'=8,'head'=4] {'seq'}, use_global_device_ids=true, to_apply=%add.3 | all-reduce | flops 272 | bytes 2176
  172.7 4.9 %copy.149 = bf16[1536,1024]{0,1:T(8,128)(2,1)} copy(bf16[1536,1024]{1,0:T(8,128)(2,1)} %param.17) | data formatting | bytes 6291456 | tf_op args[1]
  179.1 9.2 %fusion.10 = f32[12,16,128,64]{2,3,1,0:T(8,128)} fusion(f32[16,12,128]{2,0,1:T(8,128)S(1)} %copy.123, f32[16,12,128]{2,0,1:T(8,128)S(1)} %copy.121, f32[12,128,128]{2,1,0:T(8,128)S(1)} %fusion.63, pred[12,128,128]{2,1,0:T(8,128)(4,1)S(1)} %get-tuple-element.557, bf16[12,128,16,64]{1,0,3,2:T(8,128)(2,1)} %reshape_reshape.3), kind=kOutput, calls=%fused_computation.36 | convolution fusion | flops 421527552 | bytes 10616832 | tf_op jit(solution)/shard_map/hbts,bshp->bthp/dot_general | solution.py:58
  188.3 8.7 %fusion.11 = f32[12,16,128,64]{2,3,1,0:T(8,128)} fusion(f32[16,12,128]{2,0,1:T(8,128)S(1)} %copy_bitcast_fusion.1, f32[16,12,128]{2,0,1:T(8,128)S(1)} %copy.135, f32[12,128,128]{2,1,0:T(8,128)S(1)} %fusion.64, pred[12,128,128]{2,1,0:T(8,128)(4,1)S(1)} %get-tuple-element.558, bf16[1536,16,64]{0,2,1:T(8,128)(2,1)S(1)} %copy-done.1), kind=kOutput, calls=%fused_computation.37 | convolution fusion | flops 421527552 | bytes 10616832 | tf_op jit(solution)/shard_map/hbts,bshp->bthp/dot_general | solution.py:58
  198.3 52.1 %while.69 = (s32[]{:T(128)}, f32[16,128,64]{2,1,0:T(8,128)}, f32[1]{0:T(128)}, f32[1]{0:T(128)}, s32[]{:T(128)}, /*index=5*/f32[8,16,128,64]{2,3,1,0:T(8,128)}, ...) while((s32[]{:T(128)}, f32[16,128,64]{2,1,0:T(8,128)}, ...), condition=%wide.region_9.10_spmd, body=%wide.region_8.9_spmd.sunk | while | flops 262175 | bytes 3670492 | solution.py:22
  201.5 2.4 bitcast_add_fusion.10
  208.9 2.4 bitcast_add_fusion.10
  216.4 2.4 bitcast_add_fusion.10
  223.8 2.4 bitcast_add_fusion.10
  231.3 2.4 bitcast_add_fusion.10
  238.7 2.4 bitcast_add_fusion.10
  246.1 2.4 bitcast_add_fusion.10
  251.7 12.6 %fusion.24 = f32[12,16,8,8,128]{4,3,2,1,0:T(8,128)} fusion(f32[12,16,128,64]{2,3,1,0:T(8,128)} %fusion.11, f32[12,128,16]{1,2,0:T(8,128)S(1)} %copy-done.7, bf16[12,128,128,1]{2,1,3,0:T(8,128)(2,1)S(1)} %bitcast.179, f32[12,16,128,64]{3,2,1,0:T(8,128)} %get-tuple-element.305, f32[16,128,64]{2,1,0:T(8,128)S(1)} %broadcast_multiply_fusion, ...), kind=kOutput, calls=%fused_computation.54 | convolution fusion | flops 410517504 | bytes 19890944 | tf_op jit(solution)/shard_map/btn,bhnp->bthp/dot_general | solution.py:104
  264.3 6.2 %copy.179 = f32[12,16,8,8,128]{4,3,0,2,1:T(8,128)} copy(f32[12,16,8,8,128]{4,3,2,1,0:T(8,128)} %fusion.24) | data formatting | bytes 12582912 | tf_op jit(solution)/shard_map/reshape | solution.py:150
  270.5 10.3 %rev.27 = f32[1536,16,64]{0,2,1:T(8,128)} reverse(f32[1536,16,64]{0,2,1:T(8,128)} %bitcast.171), dimensions={0} | reverse | bytes 12582912 | tf_op jit(solution)/shard_map/rev | solution.py:150
  281.9 13.0 %fusion.26 = f32[12,16,8,8,128]{4,3,2,1,0:T(8,128)} fusion(f32[12,16,128,64]{2,3,1,0:T(8,128)} %fusion.10, f32[12,128,16]{1,2,0:T(8,128)} %copy.133, bf16[12,128,128,1]{2,1,3,0:T(8,128)(2,1)S(1)} %bitcast.177, f32[12,16,128,64]{3,2,1,0:T(8,128)} %get-tuple-element.299, f32[16,128,64]{2,1,0:T(8,128)} %broadcast_multiply_fusion.1, f32[12,16]{1,0:T(8,128)S(1)} %copy-done.9), kind=kOutput, calls=%fused_computation.57 | convolution fusion | flops 410517504 | bytes 19890944 | tf_op jit(solution)/shard_map/btn,bhnp->bthp/dot_general | solution.py:104
  294.9 8.5 %multiply_reduce_fusion = (f32[1536]{0:T(1024)S(1)}, f32[1536,16,64]{0,2,1:T(8,128)}) fusion(f32[16]{0:T(128)S(1)} %copy-done.14, f32[1536,16,64]{0,2,1:T(8,128)} %rev.27, f32[12,16,8,8,128]{4,3,2,1,0:T(8,128)} %fusion.26, bf16[1536,1024]{0,1:T(8,128)(2,1)} %copy.149, bf16[1536,1024]{0,1:T(8,128)(2,1)S(1)} %copy-done), kind=kLoop, calls=%fused_computation.58 | loop fusion | flops 18872832 | bytes 25172032 | tf_op jit(solution)/shard_map/reduce_sum | solution.py:158
  303.5 13.3 %all-gather.7 = f32[4,1,1536]{2,1,0:T(1,128)S(1)} all-gather(f32[1,1,1536]{2,1,0:T(1,128)S(1)} %reshape.253), channel_id=8, replica_groups=mesh['seq'=8,'head'=4] {'head'}, dimensions={0}, use_global_device_ids=true | all-gather | bytes 30720 | tf_op jit(solution)/shard_map/all_gather | solution.py:159
  316.8 3.4 %fusion.22 = bf16[1536,1024]{0,1:T(8,128)(2,1)S(1)} fusion(f32[1536,16,64]{0,2,1:T(8,128)} %get-tuple-element.538, f32[1024]{0:T(1024)S(1)} %copy-done.13, f32[1536]{0:T(1024)S(1)} %add_rsqrt_fusion), kind=kLoop, calls=%fused_computation.51 | loop fusion | flops 4718592 | bytes 9447424 | tf_op jit(solution)/shard_map/convert_element_type | solution.py:163
  320.2 2.9 copy.150
  (232 shorter events, 102.8 us)
Async XLA Ops:
  6.5 19.1 %copy-start.6 = (s32[1536]{0:T(1024)S(1)}, s32[1536]{0:T(1024)}, u32[]{:S(2)}) copy-start(s32[1536]{0:T(1024)} %param.22) | copy-start | bytes 18436
  6.5 190.5 %all-gather.11.cloned.1.call-start = ((), (), s32[]{:S(2)}) async-start(), calls=%async_computation | async-start | bytes 4718592 | tf_op jit(solution)/shard_map/all_gather | solution.py:13
  50.9 40.9 %copy-start.3 = (bf16[1536,128]{1,0:T(8,128)(2,1)S(1)}, bf16[1536,128]{1,0:T(8,128)(2,1)}, u32[]{:S(2)}) copy-start(bf16[1536,128]{1,0:T(8,128)(2,1)} %get-tuple-element.547) | copy-start | bytes 1179652
  81.7 1.4 copy-start.10
  81.7 10.1 %copy-start.8 = (f32[12,16]{1,0:T(8,128)}, f32[12,16]{1,0:T(8,128)S(1)}, u32[]{:S(2)}) copy-start(f32[12,16]{1,0:T(8,128)S(1)} %get-tuple-element.300) | copy-start | bytes 2308
  82.9 114.3 %all-gather.13.cloned.1.call-start = ((), (), s32[]{:S(2)}) async-start(), calls=%async_computation.1 | async-start | bytes 4718592 | tf_op jit(solution)/shard_map/all_gather | solution.py:13
  112.8 6.1 %copy-start.12 = (f32[16]{0:T(128)S(1)}, f32[16]{0:T(128)}, u32[]{:S(2)}) copy-start(f32[16]{0:T(128)} %custom-call.3) | copy-start | bytes 196
  118.9 33.4 %copy-start.15 = (u32[32]{0:T(128)S(1)}, u32[32]{0:T(128)}, u32[]{:S(2)}) copy-start(u32[32]{0:T(128)} %constant.122) | copy-start | bytes 388
  118.9 34.9 %copy-start.11 = (f32[16]{0:T(128)S(1)}, f32[16]{0:T(128)}, u32[]{:S(2)}) copy-start(f32[16]{0:T(128)} %copy-done.10) | copy-start | bytes 196
  118.9 52.1 %copy-start.4 = (f32[12,128,16]{1,0,2:T(8,128)S(1)}, f32[12,128,16]{1,0,2:T(8,128)}, u32[]{:S(2)}) copy-start(f32[12,128,16]{1,0,2:T(8,128)} %get-tuple-element.553) | copy-start | bytes 294916
  118.9 52.8 %copy-start.5 = (f32[12,128,16]{1,0,2:T(8,128)S(1)}, f32[12,128,16]{1,0,2:T(8,128)}, u32[]{:S(2)}) copy-start(f32[12,128,16]{1,0,2:T(8,128)} %get-tuple-element.556) | copy-start | bytes 294916
  118.9 53.5 %copy-start.2 = (bf16[1536,128]{1,0:T(8,128)(2,1)S(1)}, bf16[1536,128]{1,0:T(8,128)(2,1)}, u32[]{:S(2)}) copy-start(bf16[1536,128]{1,0:T(8,128)(2,1)} %get-tuple-element.548) | copy-start | bytes 1179652
  179.1 9.2 %copy-start.1 = (bf16[1536,16,64]{0,2,1:T(8,128)(2,1)S(1)}, bf16[1536,16,64]{0,2,1:T(8,128)(2,1)}, u32[]{:S(2)}) copy-start(bf16[1536,16,64]{0,2,1:T(8,128)(2,1)} %rev.26) | copy-start | bytes 9437188
  198.3 53.4 %copy-start.7 = (f32[12,128,16]{1,2,0:T(8,128)S(1)}, f32[12,128,16]{1,2,0:T(8,128)}, u32[]{:S(2)}) copy-start(f32[12,128,16]{1,2,0:T(8,128)} %copy.147) | copy-start | bytes 294916
  270.5 11.4 %copy-start.9 = (f32[12,16]{1,0:T(8,128)S(1)}, f32[12,16]{1,0:T(8,128)}, u32[]{:S(2)}) copy-start(f32[12,16]{1,0:T(8,128)} %copy-done.8) | copy-start | bytes 2308
  281.9 13.0 %copy-start = (bf16[1536,1024]{0,1:T(8,128)(2,1)S(1)}, bf16[1536,1024]{0,1:T(8,128)(2,1)}, u32[]{:S(2)}) copy-start(bf16[1536,1024]{0,1:T(8,128)(2,1)} %copy.124) | copy-start | bytes 9437188
  281.9 13.0 %copy-start.14 = (f32[16]{0:T(128)S(1)}, f32[16]{0:T(128)}, u32[]{:S(2)}) copy-start(f32[16]{0:T(128)} %param.21) | copy-start | bytes 196
  294.9 21.9 %copy-start.13 = (f32[1024]{0:T(1024)S(1)}, f32[1024]{0:T(1024)}, u32[]{:S(2)}) copy-start(f32[1024]{0:T(1024)} %param.23) | copy-start | bytes 12292
Sparse Core Ops, SparseCore 0:
  83.0 39.4 all-gather.10
  151.0 39.5 all-gather.12
